TPU v7x, 32 devices: a whole 2x2x4 slice. The times are simulated.
32 devices in a mesh: groups: 2 (over y), fsdp: 4 (over z), dp: 2 (over x), seq: 2 (over core).
Axes of the slice: x: 2, y: 2, z: 4, core: 2. Of those that a mesh axis runs over, the one named last changes fastest.
Arguments:
- tokens: bfloat16 [4096, 8192], P(('groups', 'fsdp', 'dp', 'seq')), parts along dimension 0, may hold values from -6 to 6
- cotangent: bfloat16 [4096, 1024], P(('groups', 'fsdp', 'dp', 'seq')), parts along dimension 0, may hold values from -6 to 6
- frozen_key_weight: bfloat16 [8192, 1024], P('fsdp'), may hold values from -0.0625 to 0.0625
- adapter_down_weight: bfloat16 [4, 16, 8192], P('fsdp', None, ('dp', 'seq')), may hold values from -0.0625 to 0.0625
- adapter_up_weight: bfloat16 [4, 16, 1024], P('fsdp', None, ('dp', 'seq')), may hold values from -0.1875 to 0.1875
- tenant_block_tiles: int32 [8], P('groups'), parts along dimension 0, may hold values from 1 to 12, 16 in all
- tenant_owner_slot: int32 [4], replicated, may hold values from 0 to 3, each once
Outputs:
- input_row_gradient: bfloat16 [4096, 8192], P(('groups', 'fsdp', 'dp', 'seq')), parts along dimension 0
- grad_down: float32 [8, 16, 8192], P(('groups', 'fsdp'), None, ('dp', 'seq')), parts along dimension 0
- grad_up: float32 [8, 16, 1024], P(('groups', 'fsdp'), None, ('dp', 'seq')), parts along dimension 0
There are 2 independent parts, one for each index of `groups`. A program takes and returns all parts, laid end to end along the dimension named above; an argument that names none is the same for every part. Nothing has to cross between parts.
Inputs may be any that keep to these rules, and one draw needn't show every extreme that they name: `tenant_block_tiles`: blocks of 128-row tiles laid end to end in tenant order, summing to 16 tiles; the largest block has exactly 12 tiles. `tenant_owner_slot`: A permutation; slot s lies on fsdp index s.
All inputs are finite; a program needn't handle non-finite values.
Results may differ from a plain program's by a relative error of at most 0.005.
Values may be sent and summed in bfloat16 or wider, within the bound.
A program may use at most 64 MiB of HBM per device.

v0:
```python
import jax
import jax.numpy as jnp
from jax import lax
from jax.sharding import PartitionSpec as P


def local(
    tokens,
    cotangent,
    frozen_key_weight,
    adapter_down_weight,
    adapter_up_weight,
    tenant_block_tiles,
    tenant_owner_slot,
):
    peer_count = lax.axis_size(("dp", "seq"))
    owner_index = lax.axis_index("fsdp")
    tenant_count = tenant_owner_slot.shape[0]
    trailing = (((1,), (1,)), ((), ()))
    leading = (((0,), (0,)), ((), ()))
    bounds = jnp.cumsum(tenant_block_tiles)
    row_first = owner_index * peer_count
    positions = row_first + jnp.arange(peer_count, dtype=jnp.int32)
    tenant = jnp.sum((bounds[None, :] <= positions[:, None]).astype(jnp.int32), axis=1)
    choose = tenant[:, None] == jnp.arange(tenant_count, dtype=jnp.int32)[None, :]
    slot_ids = jnp.sum(jnp.where(choose, tenant_owner_slot[None, :], 0), axis=1)
    select = slot_ids[:, None] == jnp.arange(tenant_count, dtype=jnp.int32)[None, :]
    all_down, all_up = (
        lax.all_gather(adapter_down_weight, "fsdp", axis=0, tiled=True),
        lax.all_gather(adapter_up_weight, "fsdp", axis=0, tiled=True),
    )
    picker = select.astype(jnp.bfloat16)
    pick_down = jnp.einsum(
        "ps,srd->prd", picker, all_down, preferred_element_type=jnp.float32
    ).astype(jnp.bfloat16)
    pick_up = jnp.einsum("ps,srk->prk", picker, all_up, preferred_element_type=jnp.float32).astype(
        jnp.bfloat16
    )
    mine_down, mine_up = (
        lax.all_to_all(pick_down, ("dp", "seq"), split_axis=0, concat_axis=2, tiled=True),
        lax.all_to_all(pick_up, ("dp", "seq"), split_axis=0, concat_axis=2, tiled=True),
    )
    down_projected = mine_down[0]
    upper_limit = mine_up[0]
    lower_limit = lax.dot_general(
        cotangent, upper_limit, trailing, preferred_element_type=jnp.float32
    ).astype(jnp.bfloat16)
    inner = lax.dot_general(
        tokens, down_projected, trailing, preferred_element_type=jnp.float32
    ).astype(jnp.bfloat16)
    adapter_part = jnp.dot(lower_limit, down_projected, preferred_element_type=jnp.float32)
    blocks = lax.dot_general(
        lax.all_gather(cotangent, "fsdp", axis=0, tiled=True),
        frozen_key_weight,
        trailing,
        preferred_element_type=jnp.float32,
    ).astype(jnp.bfloat16)
    frozen_part = lax.all_to_all(blocks, "fsdp", split_axis=0, concat_axis=1, tiled=True)
    input_row_gradient = (frozen_part.astype(jnp.float32) + adapter_part).astype(jnp.bfloat16)
    part_down = lax.dot_general(lower_limit, tokens, leading, preferred_element_type=jnp.float32)
    part_up = lax.dot_general(inner, cotangent, leading, preferred_element_type=jnp.float32)
    parts_down, parts_up = (
        lax.all_to_all(part_down[None], ("dp", "seq"), split_axis=2, concat_axis=0, tiled=True),
        lax.all_to_all(part_up[None], ("dp", "seq"), split_axis=2, concat_axis=0, tiled=True),
    )
    tile_total = jnp.sum(jnp.where(tenant_owner_slot == owner_index, tenant_block_tiles, 0)).astype(
        jnp.float32
    )
    weights_one = select.astype(jnp.float32)
    dense_down = jnp.einsum("ps,prd->srd", weights_one, parts_down, precision=lax.Precision.HIGHEST)
    dense_up = jnp.einsum("ps,prk->srk", weights_one, parts_up, precision=lax.Precision.HIGHEST)
    own_down, own_up = (
        lax.psum_scatter(dense_down, "fsdp", scatter_dimension=0, tiled=True),
        lax.psum_scatter(dense_up, "fsdp", scatter_dimension=0, tiled=True),
    )
    return (input_row_gradient, own_down / tile_total, own_up / tile_total)


def solution(mesh):
    placed = (
        P(("groups", "fsdp", "dp", "seq"), None),
        P(("groups", "fsdp", "dp", "seq"), None),
        P("fsdp", None),
        P("fsdp", None, ("dp", "seq")),
        P("fsdp", None, ("dp", "seq")),
        P("groups"),
        P(),
    )
    return jax.shard_map(
        local,
        mesh=mesh,
        in_specs=placed,
        out_specs=(
            P(("groups", "fsdp", "dp", "seq"), None),
            P(("groups", "fsdp"), None, ("dp", "seq")),
            P(("groups", "fsdp"), None, ("dp", "seq")),
        ),
        check_vma=False,
    )
```

profile of v0, /device:TPU:0, one launch (start us, length us, event | category | flops | bytes accessed | tf_op | source)
XLA Modules:
  0.0 203.2 jit_solution(18406087089155978175)
XLA Ops:
  7.9 15.0 %all_gather.10 = bf16[4,16,256]{2,1,0:T(8,128)(2,1)S(1)} all-gather(bf16[1,16,256]{2,1,0:T(8,128)(2,1)} %param.11), channel_id=1, replica_groups=mesh['groups'=2,'fsdp'=4,'dp'=2,'seq'=2] {'fsdp'}, dimensions={0}, use_global_device_ids=true | all-gather | bytes 40960 | tf_op jit(solution)/shard_map/all_gather | solution.py:30
  23.0 0.8 reduce-window.8
  24.0 0.8 select_reduce_fusion
  25.7 3.3 %all-to-all-start.1 = ((bf16[4,16,256]{2,1,0:T(8,128)(2,1)}), bf16[4,16,256]{2,1,0:T(8,128)(2,1)S(1)}, u32[]{:S(2)}, u32[]{:S(2)}) async-start(bf16[4,16,256]{2,1,0:T(8,128)(2,1)} %copy.48), calls=%async_computation.1 | async-start | bytes 65536 | tf_op jit(solution)/shard_map/all_to_all | solution.py:41
  28.9 16.7 %all_gather.11 = bf16[4,16,2048]{2,1,0:T(8,128)(2,1)S(1)} all-gather(bf16[1,16,2048]{2,1,0:T(8,128)(2,1)} %param.10), channel_id=1, replica_groups=mesh['groups'=2,'fsdp'=4,'dp'=2,'seq'=2] {'fsdp'}, dimensions={0}, use_global_device_ids=true | all-gather | bytes 327680 | tf_op jit(solution)/shard_map/all_gather | solution.py:29
  46.0 0.9 copy.52
  46.8 3.4 %all-to-all-start.2 = ((bf16[4,16,2048]{2,1,0:T(8,128)(2,1)}), bf16[4,16,2048]{2,1,0:T(8,128)(2,1)S(1)}, u32[]{:S(2)}, u32[]{:S(2)}) async-start(bf16[4,16,2048]{2,1,0:T(8,128)(2,1)} %copy.52), calls=%async_computation.2 | async-start | bytes 524288 | tf_op jit(solution)/shard_map/all_to_all | solution.py:40
  50.3 1.1 convolution_convert_fusion.3
  51.4 4.8 %all-to-all-done.2 = bf16[4,16,2048]{2,1,0:T(8,128)(2,1)S(1)} async-done(((bf16[4,16,2048]{2,1,0:T(8,128)(2,1)}), bf16[4,16,2048]{2,1,0:T(8,128)(2,1)S(1)}, u32[]{:S(2)}, u32[]{:S(2)}) %all-to-all-start.2) | async-done | bytes 262176 | tf_op jit(solution)/shard_map/all_to_all | solution.py:40
  56.7 1.0 fusion.1
  58.1 1.9 reduce.2
  60.1 0.9 reshape.52
  61.0 3.3 %all-to-all-start.4 = ((f32[4,1,4096]{2,1,0:T(1,128)}), f32[4,1,4096]{2,1,0:T(1,128)S(1)}, u32[]{:S(2)}, u32[]{:S(2)}) async-start(f32[4,1,4096]{2,1,0:T(1,128)} %reshape.52), calls=%async_computation.5 | async-start | bytes 131072 | tf_op jit(solution)/shard_map/all_to_all | solution.py:64
  64.3 2.9 %fusion.14 = f32[16,8192]{0,1:T(8,128)} fusion(bf16[16,128]{1,0:T(8,128)(2,1)S(1)} %convolution_convert_fusion.3, bf16[128,8192]{1,0:T(8,128)(2,1)S(1)} %copy-done), kind=kOutput, calls=%fused_computation.25 | convolution fusion | flops 33554432 | bytes 2625536 | tf_op jit(solution)/shard_map/dot_general | solution.py:60
  67.2 38.4 %reduce = f32[8192,16]{1,0:T(8,128)} reduce(f32[8192,1,16]{2,1,0:T(1,128)} %bitcast.60, f32[]{:T(128)} %broadcast.9), dimensions={1}, to_apply=%bitcast.43.reduce_sub_computation | reduce | bytes 1048580
  105.5 4.6 %reshape.50 = f32[4,1,32768]{2,1,0:T(1,128)} reshape(f32[8192,16]{1,0:T(8,128)} %reduce) | data formatting | bytes 1048576
  110.1 3.7 %all-to-all-start.3 = ((f32[4,1,32768]{2,1,0:T(1,128)}), f32[4,1,32768]{2,1,0:T(1,128)S(1)}, u32[]{:S(2)}, u32[]{:S(2)}) async-start(f32[4,1,32768]{2,1,0:T(1,128)} %reshape.50), calls=%async_computation.3 | async-start | bytes 1048576 | tf_op jit(solution)/shard_map/all_to_all | solution.py:63
  113.8 6.2 %convolution_convert_fusion = bf16[512,2048]{1,0:T(8,128)(2,1)} fusion(bf16[512,1024]{1,0:T(8,128)(2,1)} %all-gather.2.cloned.1.call-done, bf16[2048,1024]{1,0:T(8,128)(2,1)} %param.9), kind=kOutput, calls=%fused_computation.3 | convolution fusion | flops 2148532224 | bytes 7340032 | tf_op jit(solution)/shard_map/dot_general | solution.py:52
  120.0 2.5 %all-to-all-done.3 = f32[4,1,32768]{2,1,0:T(1,128)S(1)} async-done(((f32[4,1,32768]{2,1,0:T(1,128)}), f32[4,1,32768]{2,1,0:T(1,128)S(1)}, u32[]{:S(2)}, u32[]{:S(2)}) %all-to-all-start.3) | async-done | bytes 524320 | tf_op jit(solution)/shard_map/all_to_all | solution.py:63
  122.6 4.4 %all-to-all-start = ((bf16[4,128,2048]{2,1,0:T(8,128)(2,1)}), bf16[4,128,2048]{2,1,0:T(8,128)(2,1)}, u32[]{:S(2)}, u32[]{:S(2)}) async-start(bf16[4,128,2048]{2,1,0:T(8,128)(2,1)} %bitcast.64), calls=%async_computation | async-start | bytes 4194304 | tf_op jit(solution)/shard_map/all_to_all | solution.py:58
  127.1 0.8 reduce.3
  127.9 0.9 reshape.53
  129.9 2.1 %reduce.1 = f32[4,32768]{1,0:T(4,128)S(1)} reduce(f32[4,1,32768]{2,1,0:T(1,128)S(1)} %all-to-all-done.3, f32[]{:T(128)} %broadcast.9), dimensions={1}, to_apply=%all_to_all.66.reduce_sub_computation | reduce | bytes 1048580 | tf_op jit(solution)/shard_map/all_to_all | solution.py:63
  132.1 9.8 %reshape.51 = f32[8192,1,16]{2,1,0:T(1,128)} reshape(f32[4,32768]{1,0:T(4,128)S(1)} %reduce.1) | data formatting | bytes 1048576
  141.9 2.9 %copy.64 = f32[1,16,4,2048]{3,2,1,0:T(4,128)S(1)} copy(f32[1,16,4,2048]{1,3,2,0:T(8,128)} %bitcast.58) | data formatting | bytes 1048576 | tf_op jit(solution)/shard_map/all_to_all | solution.py:63
  145.4 1.1 copy.56
  147.8 9.0 %reduce-scatter.5.cloned.1.call-done = f32[1,16,256]{2,1,0:T(8,128)} async-done(((f32[4,16,256]{2,1,0:T(8,128)}), f32[1,16,256]{2,1,0:T(8,128)}) %reduce-scatter.5.cloned.1.call-update) | async-done | bytes 16400 | tf_op jit(solution)/shard_map/reduce_scatter | solution.py:74
  156.8 1.3 broadcast_divide_fusion.1
  158.1 32.4 %reduce-scatter.3.cloned.1.call-done = f32[1,16,2048]{2,1,0:T(8,128)} async-done(((f32[4,16,2048]{2,1,0:T(8,128)}), f32[1,16,2048]{2,1,0:T(8,128)}) %reduce-scatter.3.cloned.1.call-update) | async-done | bytes 131088 | tf_op jit(solution)/shard_map/reduce_scatter | solution.py:73
  190.5 1.6 broadcast_divide_fusion
  192.0 2.1 %convert_bitcast_fusion = f32[4,16,8,2048]{3,2,1,0:T(8,128)S(1)} fusion(bf16[4,128,2048]{2,1,0:T(8,128)(2,1)} %all-to-all-done), kind=kLoop, calls=%fused_computation.2 | loop fusion | flops 1048576 | bytes 6291456
  194.7 2.1 %fusion = bf16[128,8192]{1,0:T(8,128)(2,1)} fusion(f32[128,8192]{1,0:T(8,128)S(1)} %bitcast.59, bf16[16,128]{1,0:T(8,128)(2,1)S(1)} %convolution_convert_fusion.3, bf16[16,8192]{1,0:T(8,128)(2,1)S(1)} %bitcast.62), kind=kOutput, calls=%fused_computation.1 | convolution fusion | flops 35651584 | bytes 6557696 | tf_op jit(solution)/shard_map/dot_general | solution.py:51
  (34 shorter events, 5.9 us)
Async XLA Ops:
  7.2 49.5 %copy-start = (bf16[128,8192]{1,0:T(8,128)(2,1)S(1)}, bf16[128,8192]{1,0:T(8,128)(2,1)}, u32[]{:S(2)}) copy-start(bf16[128,8192]{1,0:T(8,128)(2,1)} %param.7) | copy-start | bytes 6291460
  7.2 49.5 %copy-start.1 = (bf16[128,1024]{1,0:T(8,128)(2,1)S(1)}, bf16[128,1024]{1,0:T(8,128)(2,1)}, u32[]{:S(2)}) copy-start(bf16[128,1024]{1,0:T(8,128)(2,1)} %param.8) | copy-start | bytes 786436
  7.2 106.6 %all-gather.2.cloned.1.call-start = ((), (), s32[]{:S(2)}) async-start(), calls=%async_computation.7 | async-start | bytes 1310720 | tf_op jit(solution)/shard_map/all_gather | solution.py:53
  25.7 21.2 %all-to-all-start.1 = ((bf16[4,16,256]{2,1,0:T(8,128)(2,1)}), bf16[4,16,256]{2,1,0:T(8,128)(2,1)S(1)}, u32[]{:S(2)}, u32[]{:S(2)}) async-start(bf16[4,16,256]{2,1,0:T(8,128)(2,1)} %copy.48), calls=%async_computation.1 | async-start | bytes 65536 | tf_op jit(solution)/shard_map/all_to_all | solution.py:41
  46.8 9.4 %all-to-all-start.2 = ((bf16[4,16,2048]{2,1,0:T(8,128)(2,1)}), bf16[4,16,2048]{2,1,0:T(8,128)(2,1)S(1)}, u32[]{:S(2)}, u32[]{:S(2)}) async-start(bf16[4,16,2048]{2,1,0:T(8,128)(2,1)} %copy.52), calls=%async_computation.2 | async-start | bytes 524288 | tf_op jit(solution)/shard_map/all_to_all | solution.py:40
  61.0 49.2 %all-to-all-start.4 = ((f32[4,1,4096]{2,1,0:T(1,128)}), f32[4,1,4096]{2,1,0:T(1,128)S(1)}, u32[]{:S(2)}, u32[]{:S(2)}) async-start(f32[4,1,4096]{2,1,0:T(1,128)} %reshape.52), calls=%async_computation.5 | async-start | bytes 131072 | tf_op jit(solution)/shard_map/all_to_all | solution.py:64
  110.1 12.4 %all-to-all-start.3 = ((f32[4,1,32768]{2,1,0:T(1,128)}), f32[4,1,32768]{2,1,0:T(1,128)S(1)}, u32[]{:S(2)}, u32[]{:S(2)}) async-start(f32[4,1,32768]{2,1,0:T(1,128)} %reshape.50), calls=%async_computation.3 | async-start | bytes 1048576 | tf_op jit(solution)/shard_map/all_to_all | solution.py:63
  122.6 69.5 %all-to-all-start = ((bf16[4,128,2048]{2,1,0:T(8,128)(2,1)}), bf16[4,128,2048]{2,1,0:T(8,128)(2,1)}, u32[]{:S(2)}, u32[]{:S(2)}) async-start(bf16[4,128,2048]{2,1,0:T(8,128)(2,1)} %bitcast.64), calls=%async_computation | async-start | bytes 4194304 | tf_op jit(solution)/shard_map/all_to_all | solution.py:58
  127.0 29.8 %reduce-scatter.5.cloned.1.call-start = ((), (), s32[]{:S(2)}) async-start(), calls=%async_computation.9 | async-start | bytes 81920 | tf_op jit(solution)/shard_map/reduce_scatter | solution.py:74
  129.9 60.6 %reduce-scatter.3.cloned.1.call-start = ((), (), s32[]{:S(2)}) async-start(), calls=%async_computation.8 | async-start | bytes 655360 | tf_op jit(solution)/shard_map/reduce_scatter | solution.py:73
  141.8 4.7 %copy-start.2 = (s32[4]{0:T(128)S(1)}, s32[4]{0:T(128)}, u32[]{:S(2)}) copy-start(s32[4]{0:T(128)} %param.13) | copy-start | bytes 52
  141.9 4.7 %copy-start.3 = (s32[4]{0:T(128)S(1)}, s32[4]{0:T(128)}, u32[]{:S(2)}) copy-start(s32[4]{0:T(128)} %param.12) | copy-start | bytes 52
Sparse Core Ops, SparseCore 0:
  9.6 34.4 all-gather.1
  130.7 26.0 reduce-scatter.4
  159.2 31.2 reduce-scatter.2
where the time goes:
time: 204 us; the launch traced here: 203 us
  other arithmetic  50.8 us (25%)
  waiting for transfers between devices  49.5 us (24%)
  blocking collectives  31.7 us (16%)
  local copies, waits for them, and re-layouts  23.9 us (12%)
  starting transfers between devices  18.2 us (9%)
  matrix products  14.6 us (7%)
  between operations  14.6 us (7%)
    unnamed x3, other arithmetic  42.4 us
    reduce_scatter x1, waiting for transfers between devices, local(): lax.psum_scatter(dense_down, 'fsdp', scatter_dimension=0, tiled=True)  32.4 us
    unnamed x15, local copies, waits for them, and re-layouts  16.9 us
    all_gather x1, blocking collectives, local(): lax.all_gather(adapter_down_weight, 'fsdp', axis=0, tiled=True)  16.7 us
    all_gather x1, blocking collectives, local(): lax.all_gather(adapter_up_weight, 'fsdp', axis=0, tiled=True)  15 us
    reduce_scatter x1, waiting for transfers between devices, local(): lax.psum_scatter(dense_up, 'fsdp', scatter_dimension=0, tiled=True)  8.97 us
    dot_general x1, matrix products, local(): lax.dot_general(lax.all_gather(cotangent, 'fsdp', axis=0, tiled=True), fr...  6.2 us
    all_to_all x1, waiting for transfers between devices, local(): lax.all_to_all(pick_down, ('dp', 'seq'), split_axis=0, concat_axis=2, til...  4.84 us
  transfers between devices with their start and end apart: 8, of which 4 were waited for; matrix products, arithmetic and copies ran while one was open for 42% of the time, Pallas kernels for 0%

commit v1 on v0

v1 whole, which is shorter than its diff:
```python
import functools

import jax
import jax.numpy as jnp
from jax import lax
from jax.experimental import pallas as pl
from jax.experimental.pallas import tpu as pltpu
from jax.sharding import PartitionSpec as P

MESH = pl.DeviceIdType.MESH
TRAILING = (((1,), (1,)), ((), ()))
LEADING = (((0,), (0,)), ((), ()))


def kernel(
    n,
    dp_size,
    seq_size,
    tiles_ref,
    owner_ref,
    tok_hbm,
    cot_hbm,
    weight_hbm,
    down_hbm,
    up_hbm,
    out_hbm,
    low_out,
    down_out,
    grad_down,
    grad_up,
    weight,
    tok,
    cot_all,
    ad_all,
    res,
    pick,
    mine,
    part_send,
    part_recv,
    sum_send,
    sum_recv,
    local_sem,
    cot_send_sem,
    cot_recv_sem,
    ad_send_sem,
    ad_recv_sem,
    res_send_sem,
    res_recv_sem,
    pick_send_sem,
    pick_recv_sem,
    part_send_sem,
    part_recv_sem,
    sum_send_sem,
    sum_recv_sem,
):
    peers = dp_size * seq_size
    z = lax.axis_index("fsdp")
    p = lax.axis_index("dp") * seq_size + lax.axis_index("seq")
    tenants = owner_ref.shape[0]
    width = weight.shape[0]
    wide = down_hbm.shape[2]
    chunk = min(512, width)

    def along(index):
        return {"fsdp": index}

    def peer(index):
        return {"dp": index // seq_size, "seq": index % seq_size}

    def remote(src, dst, send, recv, device):
        return pltpu.make_async_remote_copy(
            src_ref=src, dst_ref=dst, send_sem=send, recv_sem=recv, device_id=device, device_id_type=MESH
        )

    load_down = pltpu.make_async_copy(down_hbm.at[0], ad_all.at[z, :, pl.ds(0, wide)], local_sem.at[0])
    load_up = pltpu.make_async_copy(
        up_hbm.at[0], ad_all.at[z, :, pl.ds(wide, up_hbm.shape[2])], local_sem.at[1]
    )
    load_cot = pltpu.make_async_copy(cot_hbm, cot_all.at[z], local_sem.at[2])
    load_weight = pltpu.make_async_copy(weight_hbm, weight, local_sem.at[3])
    load_tok = pltpu.make_async_copy(tok_hbm, tok, local_sem.at[4])
    load_down.start()
    load_up.start()
    load_cot.start()
    load_weight.start()
    load_tok.start()

    barrier = pltpu.get_barrier_semaphore()
    for i in range(1, n):
        pl.semaphore_signal(barrier, inc=1, device_id=along(lax.rem(z + i, n)), device_id_type=MESH)
    for j in range(1, peers):
        pl.semaphore_signal(barrier, inc=1, device_id=peer(lax.rem(p + j, peers)), device_id_type=MESH)
    load_down.wait()
    load_up.wait()
    pl.semaphore_wait(barrier, n - 1 + peers - 1)

    def valid(direction, k):
        return (z - k >= 0) if direction == 0 else (z + k <= n - 1)

    def more(direction):
        return (z < n - 1) if direction == 0 else (z > 0)

    def onward(direction):
        return jnp.minimum(z + 1, n - 1) if direction == 0 else jnp.maximum(z - 1, 0)

    def source(direction, k):
        return jnp.maximum(z - k, 0) if direction == 0 else jnp.minimum(z + k, n - 1)

    def ad_hop(direction, k):
        block = z if k == 0 else source(direction, k)
        return remote(
            ad_all.at[block],
            ad_all.at[block],
            ad_send_sem.at[direction, k],
            ad_recv_sem.at[direction, k + 1],
            along(onward(direction)),
        )

    def cot_hop(direction, k):
        block = z if k == 0 else source(direction, k)
        return remote(
            cot_hbm if k == 0 else cot_all.at[block],
            cot_all.at[block],
            cot_send_sem.at[direction, k],
            cot_recv_sem.at[direction, k + 1],
            along(onward(direction)),
        )

    def arrived(direction, k, buffer, send, recv):
        block = source(direction, k)
        remote(
            buffer.at[block], buffer.at[block], send.at[direction, k], recv.at[direction, k], along(onward(direction))
        ).wait_recv()

    def out_columns(index):
        return out_hbm.at[:, pl.ds(pl.multiple_of(index * width, 128), width)]

    def result(direction, k):
        block = source(direction, k)
        return remote(
            res.at[block],
            out_columns(z),
            res_send_sem.at[direction, k],
            res_recv_sem.at[direction, k],
            along(block),
        )

    def product(block):
        def body(i, carry):
            at = pl.ds(pl.multiple_of(i * chunk, chunk), chunk)
            res[block, :, at] = lax.dot_general(
                cot_all[block], weight[at, :], TRAILING, preferred_element_type=jnp.float32
            ).astype(jnp.bfloat16)
            return carry

        lax.fori_loop(0, width // chunk, body, 0)

    for direction in (0, 1):

        @pl.when(more(direction))
        def _():
            ad_hop(direction, 0).start()
            cot_hop(direction, 0).start()

    load_cot.wait()
    load_weight.wait()
    product(z)
    own_out = pltpu.make_async_copy(res.at[z], out_columns(z), local_sem.at[5])
    own_out.start()

    for k in range(1, n):
        for direction in (0, 1):

            @pl.when(valid(direction, k))
            def _():
                arrived(direction, k, ad_all, ad_send_sem, ad_recv_sem)
                if k < n - 1:

                    @pl.when(more(direction))
                    def _():
                        ad_hop(direction, k).start()

                arrived(direction, k, cot_all, cot_send_sem, cot_recv_sem)
                if k < n - 1:

                    @pl.when(more(direction))
                    def _():
                        cot_hop(direction, k).start()

        for direction in (0, 1):

            @pl.when(valid(direction, k))
            def _():
                product(source(direction, k))
                result(direction, k).start()

    def slot_of(j):
        position = z * peers + lax.rem(p + j, peers)
        low, slot = jnp.int32(0), jnp.int32(0)
        for t in range(tenants):
            high = low + tiles_ref[t]
            inside = jnp.logical_and(position >= low, position < high)
            slot = slot + jnp.where(inside, owner_ref[t], 0)
            low = high
        return slot

    slots = [slot_of(j) for j in range(peers)]

    def chosen(j):
        total = None
        for s in range(n):
            term = jnp.where(slots[j] == s, 1.0, 0.0) * ad_all[s].astype(jnp.float32)
            total = term if total is None else total + term
        return total.astype(jnp.bfloat16)

    def pick_copy(j):
        return remote(
            pick.at[j], mine.at[p], pick_send_sem.at[j], pick_recv_sem.at[j], peer(lax.rem(p + j, peers))
        )

    for j in range(1, peers):
        pick[j] = chosen(j)
        pick_copy(j).start()
    mine[p] = chosen(0)
    for j in range(1, peers):
        came = lax.rem(p + peers - j, peers)
        remote(mine.at[came], mine.at[came], pick_send_sem.at[j], pick_recv_sem.at[j], peer(came)).wait_recv()

    load_tok.wait()
    low_t = jnp.zeros(low_out.shape, jnp.float32)
    inner_t = jnp.zeros(low_out.shape, jnp.float32)
    narrow = mine.shape[2] - wide
    for q in range(peers):
        low_t += lax.dot_general(
            mine[q, :, wide:],
            cot_all[z, :, q * narrow : (q + 1) * narrow],
            TRAILING,
            preferred_element_type=jnp.float32,
        )
    for q in range(peers):
        inner_t += lax.dot_general(
            mine[q, :, :wide],
            tok[:, q * wide : (q + 1) * wide],
            TRAILING,
            preferred_element_type=jnp.float32,
        )
        down_out[:, q * wide : (q + 1) * wide] = mine[q, :, :wide]
    low_t = low_t.astype(jnp.bfloat16)
    inner_t = inner_t.astype(jnp.bfloat16)
    low_out[...] = low_t

    def part_copy(j):
        return remote(
            part_send.at[j],
            part_recv.at[j],
            part_send_sem.at[j],
            part_recv_sem.at[j],
            peer(lax.rem(p + j, peers)),
        )

    def part(j, target):
        q = lax.rem(p + j, peers)
        target[j, :, :wide] = jnp.dot(
            low_t,
            tok[:, pl.ds(pl.multiple_of(q * wide, 128), wide)],
            preferred_element_type=jnp.float32,
        )
        target[j, :, wide:] = jnp.dot(
            inner_t,
            cot_all[z, :, pl.ds(pl.multiple_of(q * narrow, 128), narrow)],
            preferred_element_type=jnp.float32,
        )

    for j in range(1, peers):
        part(j, part_send)
        part_copy(j).start()
    part(0, part_recv)
    for j in range(1, peers):
        part_copy(j).wait_recv()

    def slot_sum(s):
        total = None
        for j in range(peers):
            term = jnp.where(slots[(peers - j) % peers] == s, 1.0, 0.0) * part_recv[j]
            total = term if total is None else total + term
        return total

    def sum_copy(i):
        return remote(
            sum_send.at[i], sum_recv.at[i], sum_send_sem.at[i], sum_recv_sem.at[i], along(lax.rem(z + i, n))
        )

    for i in range(1, n):
        sum_send[i] = slot_sum(lax.rem(z + i, n)).astype(jnp.bfloat16)
        sum_copy(i).start()
    total = slot_sum(z)
    for i in range(1, n):
        sum_copy(i).wait_recv()
        total = total + sum_recv[i].astype(jnp.float32)
    grad_down[...] = total[:, :wide]
    grad_up[...] = total[:, wide:]

    for k in range(1, n):
        for direction in (0, 1):
            @pl.when(valid(1 - direction, k))
            def _():
                came = source(1 - direction, k)
                remote(
                    res.at[came],
                    out_columns(came),
                    res_send_sem.at[direction, k],
                    res_recv_sem.at[direction, k],
                    along(came),
                ).wait_recv()

    own_out.wait()
    for direction in (0, 1):
        for k in range(n - 1):

            @pl.when(jnp.logical_and(more(direction), valid(direction, k)))
            def _():
                ad_hop(direction, k).wait_send()
                cot_hop(direction, k).wait_send()

        for k in range(1, n):

            @pl.when(valid(direction, k))
            def _():
                result(direction, k).wait_send()

    for j in range(1, peers):
        pick_copy(j).wait_send()
        part_copy(j).wait_send()
    for i in range(1, n):
        sum_copy(i).wait_send()


def local(
    n,
    dp_size,
    seq_size,
    tokens,
    cotangent,
    frozen_key_weight,
    adapter_down_weight,
    adapter_up_weight,
    tenant_block_tiles,
    tenant_owner_slot,
):
    peers = dp_size * seq_size
    rows, model = tokens.shape
    keys = cotangent.shape[1]
    width = frozen_key_weight.shape[0]
    _, rank, wide = adapter_down_weight.shape
    narrow = adapter_up_weight.shape[2]
    both = wide + narrow
    bf16, f32 = jnp.bfloat16, jnp.float32
    vmem = pl.BlockSpec(memory_space=pltpu.VMEM)
    smem = pl.BlockSpec(memory_space=pltpu.SMEM)
    anywhere = pl.BlockSpec(memory_space=pl.ANY)
    dma = pltpu.SemaphoreType.DMA
    frozen_part, low_t, down, sum_down, sum_up = pl.pallas_call(
        functools.partial(kernel, n, dp_size, seq_size),
        out_shape=(
            jax.ShapeDtypeStruct((rows, model), bf16),
            jax.ShapeDtypeStruct((rank, rows), bf16),
            jax.ShapeDtypeStruct((rank, model), bf16),
            jax.ShapeDtypeStruct((rank, wide), f32),
            jax.ShapeDtypeStruct((rank, narrow), f32),
        ),
        in_specs=[smem, smem, anywhere, anywhere, anywhere, anywhere, anywhere],
        out_specs=(anywhere, vmem, vmem, vmem, vmem),
        scratch_shapes=[
            pltpu.VMEM((width, keys), bf16),
            pltpu.VMEM((rows, model), bf16),
            pltpu.VMEM((n, rows, keys), bf16),
            pltpu.VMEM((n, rank, both), bf16),
            pltpu.VMEM((n, rows, width), bf16),
            pltpu.VMEM((peers, rank, both), bf16),
            pltpu.VMEM((peers, rank, both), bf16),
            pltpu.VMEM((peers, rank, both), f32),
            pltpu.VMEM((peers, rank, both), f32),
            pltpu.VMEM((n, rank, both), bf16),
            pltpu.VMEM((n, rank, both), bf16),
            dma((6,)),
            dma((2, n)),
            dma((2, n + 1)),
            dma((2, n)),
            dma((2, n + 1)),
            dma((2, n)),
            dma((2, n)),
            dma((peers,)),
            dma((peers,)),
            dma((peers,)),
            dma((peers,)),
            dma((n,)),
            dma((n,)),
        ],
        compiler_params=pltpu.CompilerParams(
            collective_id=0, has_side_effects=True, vmem_limit_bytes=56 * 1024 * 1024
        ),
        cost_estimate=pl.CostEstimate(
            flops=2 * n * rows * keys * width, bytes_accessed=16 * 1024 * 1024, transcendentals=0
        ),
    )(
        tenant_block_tiles,
        tenant_owner_slot,
        tokens,
        cotangent,
        frozen_key_weight,
        adapter_down_weight,
        adapter_up_weight,
    )
    adapter_part = lax.dot_general(low_t, down, LEADING, preferred_element_type=f32)
    input_row_gradient = (frozen_part.astype(f32) + adapter_part).astype(bf16)
    mine = tenant_owner_slot == lax.axis_index("fsdp")
    tile_total = jnp.sum(jnp.where(mine, tenant_block_tiles, 0)).astype(f32)
    return (input_row_gradient, (sum_down / tile_total)[None], (sum_up / tile_total)[None])


def solution(mesh):
    placed = (
        P(("groups", "fsdp", "dp", "seq"), None),
        P(("groups", "fsdp", "dp", "seq"), None),
        P("fsdp", None),
        P("fsdp", None, ("dp", "seq")),
        P("fsdp", None, ("dp", "seq")),
        P("groups"),
        P(),
    )
    sizes = (mesh.shape["fsdp"], mesh.shape["dp"], mesh.shape["seq"])
    return jax.shard_map(
        functools.partial(local, *sizes),
        mesh=mesh,
        in_specs=placed,
        out_specs=(
            P(("groups", "fsdp", "dp", "seq"), None),
            P(("groups", "fsdp"), None, ("dp", "seq")),
            P(("groups", "fsdp"), None, ("dp", "seq")),
        ),
        check_vma=False,
    )
```

time: 204 us -> 82.2 us (0.40)
  Pallas kernels: 0 us -> 75 us
  waiting for transfers between devices: 49.5 us -> 0 us
  other arithmetic: 50.8 us -> 1.92 us
  blocking collectives: 31.7 us -> 0 us
  local copies, waits for them, and re-layouts: 23.9 us -> 0.02 us
  starting transfers between devices: 18.2 us -> 0 us
  between operations: 14.6 us -> 1.33 us
  matrix products: 14.6 us -> 3.78 us
    pallas_call x0 -> x1, Pallas kernels: none -> 75 us  [local(): pl.pallas_call(functools.partial(kernel, n, dp_size, seq_size), out_shape...]
    unnamed x3 -> x0, other arithmetic: 42.4 us -> none
    reduce_scatter x2 -> x0, waiting for transfers between devices: 41.3 us -> none  [the longest x1 32.4 us: local(): lax.psum_scatter(dense_down, 'fsdp', scatter_dimension=0, tiled=True)]
    all_gather x2 -> x0, blocking collectives: 31.7 us -> none  [the longest x1 16.7 us: local(): lax.all_gather(adapter_down_weight, 'fsdp', axis=0, tiled=True)]
    all_to_all x5 -> x0, starting transfers between devices: 18.1 us -> none  [the longest x1 4.45 us: local(): lax.all_to_all(blocks, 'fsdp', split_axis=0, concat_axis=1, tiled=True)]
    unnamed x15 -> x8, local copies, waits for them, and re-layouts: 16.9 us -> 0.02 us
    dot_general x9 -> x1, matrix products: 14.6 us -> 3.78 us  [local(): lax.dot_general(low_t, down, LEADING, preferred_element_type=f32)]
    all_to_all x5 -> x0, waiting for transfers between devices: 7.39 us -> none  [the longest x1 4.84 us: local(): lax.all_to_all(pick_down, ('dp', 'seq'), split_axis=0, concat_axis=2, til...]
  transfers between devices with their start and end apart: 8 -> 0, of which waited for: 4 -> 0; matrix products, arithmetic and copies ran while one was open for 42% -> 0% of each run, Pallas kernels for 0% -> 0%
where the time goes in v1:
time: 82.2 us; the launch traced here: 82.1 us
  Pallas kernels  75 us (91%)
  matrix products  3.78 us (5%)
  other arithmetic  1.92 us (2%)
  between operations  1.33 us (2%)
    pallas_call x1, Pallas kernels, local(): pl.pallas_call(functools.partial(kernel, n, dp_size, seq_size), out_shape...  75 us
    dot_general x1, matrix products, local(): lax.dot_general(low_t, down, LEADING, preferred_element_type=f32)  3.78 us

profile of v1, /device:TPU:0, one launch (start us, length us, event | category | flops | bytes accessed | tf_op | source)
XLA Modules:
  0.0 82.1 jit_solution(13340169958421049451)
XLA Ops:
  0.6 75.0 %shard_map.94 = (bf16[128,8192]{1,0:T(8,128)(2,1)}, bf16[16,128]{1,0:T(8,128)(2,1)}, bf16[16,8192]{1,0:T(8,128)(2,1)}, f32[16,2048]{1,0:T(8,128)}, f32[16,256]{1,0:T(8,128)}) custom-call(s32[4]{0:T(128)} %tiles_ref.1, s32[4]{0:T(128)} %owner_ref.1, bf16[128,8192]{1,0:T(8,128)(2,1)} %tok_hbm.1, bf16[128,1024]{1,0:T(8,128)(2,1)} %cot_hbm.1, ...), custom_call_target="tpu_custom_call" | custom-call | flops 2147483648 | bytes 16777216 | tf_op jit(solution)/shard_map/pallas_call | solution.py:362
  75.6 0.0 copy-start.2
  75.7 0.0 copy-start.3
  75.7 0.0 copy-start
  75.7 0.0 copy-start.1
  75.7 3.8 %fusion = bf16[128,8192]{1,0:T(8,128)(2,1)} fusion(bf16[16,128]{1,0:T(8,128)(2,1)} %get-tuple-element.9, bf16[16,8192]{1,0:T(8,128)(2,1)} %get-tuple-element.10, bf16[128,8192]{1,0:T(8,128)(2,1)} %get-tuple-element.8), kind=kOutput, calls=%fused_computation.1 | convolution fusion | flops 36700160 | bytes 4460544 | tf_op jit(solution)/shard_map/dot_general | solution.py:414
  79.5 0.0 copy-done.2
  79.5 0.0 copy-done.3
  79.5 0.6 fusion.1
  80.8 0.0 copy-done
  80.8 0.7 divide_bitcast_fusion
  81.4 0.0 copy-done.1
  81.4 0.6 divide_bitcast_fusion.1
Async XLA Ops:
  75.6 3.8 %copy-start.2 = (s32[4]{0:T(128)S(1)}, s32[4]{0:T(128)}, u32[]{:S(2)}) copy-start(s32[4]{0:T(128)} %tiles_ref.1) | copy-start | bytes 52
  75.7 3.8 %copy-start.3 = (s32[4]{0:T(128)S(1)}, s32[4]{0:T(128)}, u32[]{:S(2)}) copy-start(s32[4]{0:T(128)} %owner_ref.1) | copy-start | bytes 52
  75.7 5.1 %copy-start = (f32[16,2048]{1,0:T(8,128)S(1)}, f32[16,2048]{1,0:T(8,128)}, u32[]{:S(2)}) copy-start(f32[16,2048]{1,0:T(8,128)} %get-tuple-element.11) | copy-start | bytes 393220
  75.7 5.8 %copy-start.1 = (f32[16,256]{1,0:T(8,128)S(1)}, f32[16,256]{1,0:T(8,128)}, u32[]{:S(2)}) copy-start(f32[16,256]{1,0:T(8,128)} %get-tuple-element.12) | copy-start | bytes 49156

commit v2 on v1

--- a/solution.py
+++ b/solution.py
@@ -187,9 +187,9 @@
                     def _():
                         cot_hop(direction, k).start()
 
-        for direction in (0, 1):
-
-            @pl.when(valid(direction, k))
+        for direction, now in ((1, z < n // 2), (0, z >= 0), (1, z >= n // 2)):
+
+            @pl.when(jnp.logical_and(valid(direction, k), now))
             def _():
                 product(source(direction, k))
                 result(direction, k).start()
@@ -297,8 +297,12 @@
     for i in range(1, n):
         sum_copy(i).wait_recv()
         total = total + sum_recv[i].astype(jnp.float32)
-    grad_down[...] = total[:, :wide]
-    grad_up[...] = total[:, wide:]
+    count = jnp.int32(0)
+    for t in range(tenants):
+        count = count + jnp.where(owner_ref[t] == z, tiles_ref[t], 0)
+    total = total / count.astype(jnp.float32)
+    grad_down[0] = total[:, :wide]
+    grad_up[0] = total[:, wide:]
 
     for k in range(1, n):
         for direction in (0, 1):
@@ -359,14 +363,14 @@
     smem = pl.BlockSpec(memory_space=pltpu.SMEM)
     anywhere = pl.BlockSpec(memory_space=pl.ANY)
     dma = pltpu.SemaphoreType.DMA
-    frozen_part, low_t, down, sum_down, sum_up = pl.pallas_call(
+    frozen_part, low_t, down, mean_down, mean_up = pl.pallas_call(
         functools.partial(kernel, n, dp_size, seq_size),
         out_shape=(
             jax.ShapeDtypeStruct((rows, model), bf16),
             jax.ShapeDtypeStruct((rank, rows), bf16),
             jax.ShapeDtypeStruct((rank, model), bf16),
-            jax.ShapeDtypeStruct((rank, wide), f32),
-            jax.ShapeDtypeStruct((rank, narrow), f32),
+            jax.ShapeDtypeStruct((1, rank, wide), f32),
+            jax.ShapeDtypeStruct((1, rank, narrow), f32),
         ),
         in_specs=[smem, smem, anywhere, anywhere, anywhere, anywhere, anywhere],
         out_specs=(anywhere, vmem, vmem, vmem, vmem),
@@ -413,9 +417,7 @@
     )
     adapter_part = lax.dot_general(low_t, down, LEADING, preferred_element_type=f32)
     input_row_gradient = (frozen_part.astype(f32) + adapter_part).astype(bf16)
-    mine = tenant_owner_slot == lax.axis_index("fsdp")
-    tile_total = jnp.sum(jnp.where(mine, tenant_block_tiles, 0)).astype(f32)
-    return (input_row_gradient, (sum_down / tile_total)[None], (sum_up / tile_total)[None])
+    return (input_row_gradient, mean_down, mean_up)
 
 
 def solution(mesh):

time: 82.2 us -> 80.9 us (0.984)
  other arithmetic: 1.92 us -> 0 us
  local copies, waits for them, and re-layouts: 0.02 us -> 1.27 us
    broadcast_in_dim x2 -> x0, other arithmetic: 1.29 us -> none  [the longest x1 0.67 us: local(): (sum_down / tile_total)[None]]
    unnamed x8 -> x6, local copies, waits for them, and re-layouts: 0.02 us -> 1.27 us
where the time goes in v2:
time: 80.9 us; the launch traced here: 80.7 us
  Pallas kernels  75 us (93%)
  matrix products  3.78 us (5%)
  local copies, waits for them, and re-layouts  1.27 us (2%)
    pallas_call x1, Pallas kernels, local(): pl.pallas_call(functools.partial(kernel, n, dp_size, seq_size), out_shape...  75 us
    dot_general x1, matrix products, local(): lax.dot_general(low_t, down, LEADING, preferred_element_type=f32)  3.78 us

profile of v2, /device:TPU:0, one launch (start us, length us, event | category | flops | bytes accessed | tf_op | source)
XLA Modules:
  0.0 80.7 jit_solution(18207539900638840498)
XLA Ops:
  0.6 75.0 %shard_map.94 = (bf16[128,8192]{1,0:T(8,128)(2,1)}, bf16[16,128]{1,0:T(8,128)(2,1)}, bf16[16,8192]{1,0:T(8,128)(2,1)}, f32[1,16,2048]{2,1,0:T(8,128)}, f32[1,16,256]{2,1,0:T(8,128)}) custom-call(s32[4]{0:T(128)} %tiles_ref.1, s32[4]{0:T(128)} %owner_ref.1, bf16[128,8192]{1,0:T(8,128)(2,1)} %tok_hbm.1, bf16[128,1024]{1,0:T(8,128)(2,1)} %cot_hbm.1, ...), custom_call_target="tpu_custom_call" | custom-call | flops 2147483648 | bytes 16777216 | tf_op jit(solution)/shard_map/pallas_call | solution.py:366
  75.7 0.0 copy-start
  75.7 0.0 copy-start.1
  75.7 3.8 %fusion = bf16[128,8192]{1,0:T(8,128)(2,1)} fusion(bf16[16,128]{1,0:T(8,128)(2,1)} %get-tuple-element.9, bf16[16,8192]{1,0:T(8,128)(2,1)} %get-tuple-element.10, bf16[128,8192]{1,0:T(8,128)(2,1)} %get-tuple-element.8), kind=kOutput, calls=%fused_computation.1 | convolution fusion | flops 36700160 | bytes 4460544 | tf_op jit(solution)/shard_map/dot_general | solution.py:418
  79.4 0.0 copy-done
  79.5 0.7 copy.12
  80.1 0.0 copy-done.1
  80.1 0.6 copy.13
Async XLA Ops:
  75.7 3.8 %copy-start = (f32[1,16,2048]{2,1,0:T(8,128)S(1)}, f32[1,16,2048]{2,1,0:T(8,128)}, u32[]{:S(2)}) copy-start(f32[1,16,2048]{2,1,0:T(8,128)} %get-tuple-element.17) | copy-start | bytes 393220
  75.7 4.4 %copy-start.1 = (f32[1,16,256]{2,1,0:T(8,128)S(1)}, f32[1,16,256]{2,1,0:T(8,128)}, u32[]{:S(2)}) copy-start(f32[1,16,256]{2,1,0:T(8,128)} %get-tuple-element.18) | copy-start | bytes 49156

commit v3 on v2

--- a/solution.py
+++ b/solution.py
@@ -180,6 +180,11 @@
                     def _():
                         ad_hop(direction, k).start()
 
+    def step(k):
+        for direction in (0, 1):
+
+            @pl.when(valid(direction, k))
+            def _():
                 arrived(direction, k, cot_all, cot_send_sem, cot_recv_sem)
                 if k < n - 1:
 
@@ -222,6 +227,7 @@
         pick[j] = chosen(j)
         pick_copy(j).start()
     mine[p] = chosen(0)
+    step(1)
     for j in range(1, peers):
         came = lax.rem(p + peers - j, peers)
         remote(mine.at[came], mine.at[came], pick_send_sem.at[j], pick_recv_sem.at[j], peer(came)).wait_recv()
@@ -275,6 +281,8 @@
         part(j, part_send)
         part_copy(j).start()
     part(0, part_recv)
+    for k in range(2, n):
+        step(k)
     for j in range(1, peers):
         part_copy(j).wait_recv()
 

time: 80.9 us -> 80.6 us (level)
  no operation moved by 1% of the time
where the time goes in v3:
time: 80.6 us; the launch traced here: 80.4 us
  Pallas kernels  74.7 us (93%)
  matrix products  3.77 us (5%)
  local copies, waits for them, and re-layouts  1.27 us (2%)
    pallas_call x1, Pallas kernels, local(): pl.pallas_call(functools.partial(kernel, n, dp_size, seq_size), out_shape...  74.7 us
    dot_general x1, matrix products, local(): lax.dot_general(low_t, down, LEADING, preferred_element_type=f32)  3.77 us

profile of v3, /device:TPU:0, one launch (start us, length us, event | category | flops | bytes accessed | tf_op | source)
XLA Modules:
  0.0 80.4 jit_solution(3261139157183607532)
XLA Ops:
  0.6 74.7 %shard_map.94 = (bf16[128,8192]{1,0:T(8,128)(2,1)}, bf16[16,128]{1,0:T(8,128)(2,1)}, bf16[16,8192]{1,0:T(8,128)(2,1)}, f32[1,16,2048]{2,1,0:T(8,128)}, f32[1,16,256]{2,1,0:T(8,128)}) custom-call(s32[4]{0:T(128)} %tiles_ref.1, s32[4]{0:T(128)} %owner_ref.1, bf16[128,8192]{1,0:T(8,128)(2,1)} %tok_hbm.1, bf16[128,1024]{1,0:T(8,128)(2,1)} %cot_hbm.1, ...), custom_call_target="tpu_custom_call" | custom-call | flops 2147483648 | bytes 16777216 | tf_op jit(solution)/shard_map/pallas_call | solution.py:374
  75.4 0.0 copy-start
  75.4 0.0 copy-start.1
  75.4 3.8 %fusion = bf16[128,8192]{1,0:T(8,128)(2,1)} fusion(bf16[16,128]{1,0:T(8,128)(2,1)} %get-tuple-element.9, bf16[16,8192]{1,0:T(8,128)(2,1)} %get-tuple-element.10, bf16[128,8192]{1,0:T(8,128)(2,1)} %get-tuple-element.8), kind=kOutput, calls=%fused_computation.1 | convolution fusion | flops 36700160 | bytes 4460544 | tf_op jit(solution)/shard_map/dot_general | solution.py:426
  79.1 0.0 copy-done
  79.1 0.7 copy.12
  79.8 0.0 copy-done.1
  79.8 0.6 copy.13
Async XLA Ops:
  75.4 3.8 %copy-start = (f32[1,16,2048]{2,1,0:T(8,128)S(1)}, f32[1,16,2048]{2,1,0:T(8,128)}, u32[]{:S(2)}) copy-start(f32[1,16,2048]{2,1,0:T(8,128)} %get-tuple-element.17) | copy-start | bytes 393220
  75.4 4.4 %copy-start.1 = (f32[1,16,256]{2,1,0:T(8,128)S(1)}, f32[1,16,256]{2,1,0:T(8,128)}, u32[]{:S(2)}) copy-start(f32[1,16,256]{2,1,0:T(8,128)} %get-tuple-element.18) | copy-start | bytes 49156
